TPU v7x, 256 devices: a whole 4x4x8 slice. The times are simulated.
256 devices in a mesh: fsdp: 8 (over z), tp: 8 (over x, core), rep: 4 (over y).
Axes of the slice: x: 4, y: 4, z: 8, core: 2. Of those that a mesh axis runs over, the one named last changes fastest.
Arguments:
- weight: float32 [4096, 16384], P('fsdp', 'tp'), may hold values from -6 to 6
- momentum: float32 [4, 4096, 16384], P('rep', 'fsdp', 'tp'), may hold values from -24 to 24
- gradient: bfloat16 [4, 4096, 16384], P('rep', 'fsdp', 'tp'), may hold values from -6 to 6
- q_in: float32 [16384, 128], P('tp'), may hold values from -6 to 6
Outputs:
- weight_new: float32 [4096, 16384], P('fsdp', 'tp')
- momentum_new: float32 [4, 4096, 16384], P('rep', 'fsdp', 'tp')
- q_new: float32 [16384, 128], P('tp')
All inputs are finite; a program needn't handle non-finite values.
Results may differ from a plain program's by a relative error of at most 0.0003.
Values sent between devices are 32-bit elements; how exact they have to be, the bound alone decides.
A program may use at most 64 MiB of HBM per device.

v0:
```python
import jax
import jax.numpy as jnp
from jax import lax
from jax.sharding import PartitionSpec as P


def transposed(block, basis):
    return lax.dot_general(
        block,
        basis,
        (((0,), (0,)), ((), ())),
        precision=lax.Precision.HIGHEST,
        preferred_element_type=jnp.float32,
    )


def shards(weight, momentum, gradient, q_in):
    high = lax.Precision.HIGHEST
    replicas = lax.axis_size("rep")
    columns = lax.axis_size("tp") * q_in.shape[0]
    buffer = momentum[0] + gradient[0].astype(jnp.float32)
    partial_left = jnp.dot(buffer, q_in, precision=high, preferred_element_type=jnp.float32)
    projected = lax.psum(partial_left, ("tp", "rep"))
    projected = projected / replicas
    gram = lax.psum(
        jnp.dot(projected.T, projected, precision=high, preferred_element_type=jnp.float32), "fsdp"
    )
    lower = jnp.linalg.cholesky(gram)
    basis = jax.scipy.linalg.solve_triangular(lower, projected.T, lower=True).T
    right = lax.psum(transposed(buffer, basis), ("fsdp", "rep")) / replicas
    squares = lax.psum(jnp.sum(right * right, axis=0), "tp")
    q_new = right * lax.rsqrt(squares / columns + 1e-06)
    feedback = jnp.dot(basis, right.T, precision=high, preferred_element_type=jnp.float32)
    momentum_new = (buffer - 0.05 * feedback)[None]
    weight_new = 0.999 * weight - 0.2 * jnp.dot(
        basis, q_new.T, precision=high, preferred_element_type=jnp.float32
    )
    return (weight_new, momentum_new, q_new)


def solution(mesh):
    placed = (P("fsdp", "tp"), P("rep", "fsdp", "tp"), P("rep", "fsdp", "tp"), P("tp", None))
    return jax.shard_map(
        shards,
        mesh=mesh,
        in_specs=placed,
        out_specs=(P("fsdp", "tp"), P("rep", "fsdp", "tp"), P("tp", None)),
        check_vma=False,
    )
```

profile of v0, /device:TPU:32, one launch (start us, length us, event | category | flops | bytes accessed | tf_op | source)
XLA Modules:
  0.0 420.8 jit_solution(16850036571538356375)
XLA Ops:
  7.2 0.0 all-reduce.4.cloned.1.call-start
  7.2 1.2 copy-done
  8.4 6.2 %fusion.2 = f32[512,128]{1,0:T(8,128)} fusion(f32[2048,128]{1,0:T(8,128)S(1)} %copy-done, f32[1,512,2048]{2,1,0:T(8,128)} %param.5, bf16[1,512,2048]{2,1,0:T(8,128)(2,1)} %param.6), kind=kOutput, calls=%fused_computation.3 | convolution fusion | flops 1612709888 | bytes 7602176 | tf_op jit(solution)/shard_map/dot_general | solution.py:22
  14.6 0.0 all-reduce.4.cloned.1.call-update
  14.6 0.0 all-reduce.6.cloned.1.call-start
  14.6 114.2 %all-reduce.4.cloned.1.call-done = f32[512,128]{1,0:T(8,128)} async-done(((f32[512,128]{1,0:T(8,128)}), f32[512,128]{1,0:T(8,128)}) %all-reduce.4.cloned.1.call-update) | async-done | bytes 262160 | tf_op jit(solution)/shard_map/psum | solution.py:23
  128.8 2.3 fusion.9
  131.1 0.2 all-reduce.8.cloned.1.call-start
  131.4 71.4 %all-reduce.6.cloned.1.call-done = f32[128,128]{0,1:T(8,128)} async-done(((f32[128,128]{0,1:T(8,128)}), f32[128,128]{0,1:T(8,128)}) %all-reduce.6.cloned.1.call-update) | async-done | bytes 65552 | tf_op jit(solution)/shard_map/psum | solution.py:25
  202.8 0.9 copy.8
  203.7 0.9 fusion.15
  204.6 11.7 %cholesky.16 = f32[128,128]{1,0:T(8,128)S(1)} custom-call(f32[128,128]{1,0:T(8,128)S(1)} %fusion.15), custom_call_target="Cholesky" | custom-call | tf_op jit(solution)/shard_map/jit(cholesky)/cholesky | solution.py:28
  216.3 0.6 compare_reduce_fusion
  217.0 0.7 fusion.13
  217.6 9.8 %custom-call.7 = f32[1,128,128]{1,2,0:T(8,128)S(1)} custom-call(f32[1,128,128]{2,1,0:T(8,128)S(1)} %fusion.13), custom_call_target="InvertDiagBlocksLowerTriangular" | custom-call | tf_op jit(solution)/shard_map/jit(_solve_triangular)/triangular_solve | solution.py:29
  227.4 1.4 fusion.7
  228.8 10.1 %fusion = f32[2048,128]{1,0:T(8,128)} fusion(f32[128,512]{1,0:T(8,128)S(1)} %fusion.7, f32[1,512,2048]{2,1,0:T(8,128)} %param.5, bf16[1,512,2048]{2,1,0:T(8,128)(2,1)S(1)} %copy-done.2), kind=kOutput, calls=%fused_computation.1 | convolution fusion | flops 1612709888 | bytes 7602176 | tf_op jit(solution)/shard_map/dot_general | solution.py:8
  238.9 0.0 all-reduce.8.cloned.1.call-update
  238.9 147.3 %all-reduce.8.cloned.1.call-done = f32[2048,128]{1,0:T(8,128)} async-done(((f32[2048,128]{1,0:T(8,128)}), f32[2048,128]{1,0:T(8,128)}) %all-reduce.8.cloned.1.call-update) | async-done | bytes 1048592 | tf_op jit(solution)/shard_map/psum | solution.py:30
  386.2 1.5 multiply_reduce_fusion
  387.8 12.4 %psum.31 = f32[128]{0:T(128)S(1)} all-reduce(f32[128]{0:T(128)S(1)} %multiply_reduce_fusion), channel_id=1, replica_groups=mesh['fsdp'=8,'tp'=8,'rep'=4] {'tp'}, use_global_device_ids=true, to_apply=%region_6.7 | all-reduce | flops 128 | bytes 1024 | tf_op jit(solution)/shard_map/psum | solution.py:31
  400.2 1.3 broadcast_multiply_fusion
  401.5 7.3 %multiply_subtract_fusion = f32[512,2048]{1,0:T(8,128)} fusion(f32[512,2048]{1,0:T(8,128)} %param.4, f32[128,512]{1,0:T(8,128)S(1)} %fusion.7, f32[2048,128]{1,0:T(8,128)S(1)} %broadcast_multiply_fusion), kind=kOutput, calls=%fused_computation.6 | convolution fusion | flops 1613758464 | bytes 9699328 | tf_op jit(solution)/shard_map/dot_general | solution.py:35
  408.8 5.4 %fusion.4 = f32[1,512,2048]{2,1,0:T(8,128)} fusion(f32[128,512]{1,0:T(8,128)S(1)} %fusion.7, f32[1,512,2048]{2,1,0:T(8,128)S(1)} %copy-done.1, bf16[1,512,2048]{2,1,0:T(8,128)(2,1)S(1)} %copy-done.2, f32[2048,128]{1,0:T(8,128)S(1)} %copy-done.3), kind=kOutput, calls=%fused_computation.5 | convolution fusion | flops 1615069184 | bytes 11796480 | tf_op jit(solution)/shard_map/dot_general | solution.py:33
  (12 shorter events, 0.1 us)
Async XLA Ops:
  7.2 1.2 copy-start
  7.2 221.6 %copy-start.2 = (bf16[1,512,2048]{2,1,0:T(8,128)(2,1)S(1)}, bf16[1,512,2048]{2,1,0:T(8,128)(2,1)}, u32[]{:S(2)}) copy-start(bf16[1,512,2048]{2,1,0:T(8,128)(2,1)} %param.6) | copy-start | bytes 6291460
  7.2 121.6 %all-reduce.4.cloned.1.call-start = ((), (), s32[]{:S(2)}) async-start(), calls=%async_computation | async-start | bytes 524288 | tf_op jit(solution)/shard_map/psum | solution.py:23
  14.6 188.2 %all-reduce.6.cloned.1.call-start = ((), (), s32[]{:S(2)}) async-start(), calls=%async_computation.1 | async-start | bytes 131072 | tf_op jit(solution)/shard_map/psum | solution.py:25
  131.1 255.1 %all-reduce.8.cloned.1.call-start = ((), (), s32[]{:S(2)}) async-start(), calls=%async_computation.2 | async-start | bytes 2097152 | tf_op jit(solution)/shard_map/psum | solution.py:30
  401.5 7.3 %copy-start.4 = (f32[2048,128]{1,0:T(8,128)}, f32[2048,128]{1,0:T(8,128)S(1)}, u32[]{:S(2)}) copy-start(f32[2048,128]{1,0:T(8,128)S(1)} %broadcast_multiply_fusion) | copy-start | bytes 3145732
  401.5 7.3 %copy-start.1 = (f32[1,512,2048]{2,1,0:T(8,128)S(1)}, f32[1,512,2048]{2,1,0:T(8,128)}, u32[]{:S(2)}) copy-start(f32[1,512,2048]{2,1,0:T(8,128)} %param.5) | copy-start | bytes 12582916
  401.5 7.3 %copy-start.3 = (f32[2048,128]{1,0:T(8,128)S(1)}, f32[2048,128]{1,0:T(8,128)}, u32[]{:S(2)}) copy-start(f32[2048,128]{1,0:T(8,128)} %all-reduce.8.cloned.1.call-done) | copy-start | bytes 3145732
Sparse Core Ops, SparseCore 0:
  14.7 114.0 all-reduce.3
  131.8 70.9 all-reduce.5
  239.1 147.1 all-reduce.7
where the time goes:
time: 423 us; the launch traced here: 421 us
  waiting for transfers between devices  333 us (79%)
  matrix products  32.6 us (8%)
  other arithmetic  26.5 us (6%)
  between operations  13.8 us (3%)
  blocking collectives  12.4 us (3%)
    psum x1, waiting for transfers between devices, shards(): right = lax.psum(transposed(buffer, basis), ('fsdp', 'rep')) / replicas  147 us
    psum x1, waiting for transfers between devices, shards(): projected = lax.psum(partial_left, ('tp', 'rep'))  114 us
    psum x1, waiting for transfers between devices, shards(): lax.psum(jnp.dot(projected.T, projected, precision=high, preferred_elemen...  71.4 us
    psum x1, blocking collectives, shards(): squares = lax.psum(jnp.sum(right * right, axis=0), 'tp')  12.4 us
    another operation x3, other arithmetic, shards(): lower = jnp.linalg.cholesky(gram)  12.4 us
    another operation x2, other arithmetic, shards(): basis = jax.scipy.linalg.solve_triangular(lower, projected.T, lower=True).T  10.5 us
    dot_general x1, matrix products, transposed(): lax.dot_general(block, basis, (((0,), (0,)), ((), ())), precision=lax.Pre...  10.1 us
  transfers between devices with their start and end apart: 3, of which 3 were waited for; matrix products, arithmetic and copies ran while one was open for 0% of the time, Pallas kernels for 0%

commit v1 on v0

v1 whole, which is shorter than its diff:
```python
import jax
import jax.numpy as jnp
from jax import lax
from jax.experimental import pallas as pl
from jax.experimental.pallas import tpu as pltpu
from jax.sharding import PartitionSpec as P

MESH = pl.DeviceIdType.MESH
F32 = jnp.float32
BF16 = jnp.bfloat16
Z, T, Y = 8, 8, 4
G = T * Y


def split(x):
    hi = x.astype(BF16)
    return hi, (x - hi.astype(F32)).astype(BF16)


def mm(a, b, dims=((1,), (0,))):
    return lax.dot_general(a, b, (dims, ((), ())), preferred_element_type=F32)


def mmf(a, b, dims=((1,), (0,))):
    return lax.dot_general(a, b, (dims, ((), ())), precision=lax.Precision.HIGHEST, preferred_element_type=F32)


class Exchange:
    def __init__(self, n, me, device, src, dst, send, recv):
        self.n, self.me, self.device, self.src, self.dst = n, me, device, src, dst
        self.send, self.recv = send, recv

    def each(self, body):
        def step(o, carry):
            body(lax.rem(self.me + o, self.n))
            return carry

        lax.fori_loop(1, self.n, step, 0)

    def copy(self, j, slot):
        return pltpu.make_async_remote_copy(
            src_ref=self.src(j),
            dst_ref=self.dst(slot),
            send_sem=self.send.at[j],
            recv_sem=self.recv.at[slot],
            device_id=self.device(j),
            device_id_type=MESH,
        )

    def start(self):
        self.each(lambda j: self.copy(j, self.me).start())

    def wait_recv(self):
        self.each(lambda j: self.copy(j, j).wait_recv())

    def wait_send(self):
        self.each(lambda j: self.copy(j, self.me).wait_send())


def total(ref, n):
    acc = ref[0]
    for k in range(1, n):
        acc = acc + ref[k]
    return acc


def factor(work, gram):
    rows = lax.broadcasted_iota(jnp.int32, (128, 128), 0)
    lanes = lax.broadcasted_iota(jnp.int32, (128, 128), 1)
    work[:, 0:128] = gram
    work[:, 128:256] = jnp.where(rows == lanes, 1.0, 0.0).astype(F32)

    def pivot(j, carry):
        row = work[pl.ds(j, 1), :]
        left = work[:, 0:128]
        col = jnp.sum(jnp.where(lanes == j, left, 0.0), axis=1, keepdims=True)
        d = jnp.sum(jnp.where(lanes[0:1] == j, row[:, 0:128], 0.0), axis=1, keepdims=True)
        m = jnp.where(rows[:, 0:1] > j, col * (1.0 / d), 0.0)
        work[...] = work[...] - m * row
        return carry

    lax.fori_loop(0, 128, pivot, 0)
    d = jnp.sum(jnp.where(rows == lanes, work[:, 0:128], 0.0), axis=1, keepdims=True)
    return work[:, 128:256] * lax.rsqrt(d)


def talk(
    mom, grad, q_in, right_out, basis_out, sq_out,
    mom_v, grad_v, q_v, hi_v, lo_v, q_hl,
    part, part_r, proj, gram_p, gram_r, gram,
    wa, wb, ra1, rb1, sa1, sb1, ra2, rb2, rta, rtb,
    work, basis_v, sq_t, sq_y, sq_z,
    load, store, s_tp, r_tp, s_z, r_z, s_y, r_y,
):
    f, t, r = lax.axis_index("fsdp"), lax.axis_index("tp"), lax.axis_index("rep")
    g = t * Y + r

    loads = [pltpu.make_async_copy(q_in, q_v, load.at[8])]
    for c in range(4):
        cols = pl.ds(512 * c, 512)
        loads.append(pltpu.make_async_copy(mom.at[:, cols], mom_v.at[:, cols], load.at[2 * c]))
        loads.append(pltpu.make_async_copy(grad.at[:, cols], grad_v.at[:, cols], load.at[2 * c + 1]))
    for cp in loads:
        cp.start()

    plane = lambda j: {"tp": lax.div(j, Y), "rep": lax.rem(j, Y)}
    along_z = lambda j: {"fsdp": j}
    along_y = lambda j: {"rep": j}
    along_t = lambda j: {"tp": j}

    barrier = pltpu.get_barrier_semaphore()

    def greet(n, me, device):
        def step(o, carry):
            pl.semaphore_signal(barrier, inc=1, device_id=device(lax.rem(me + o, n)), device_id_type=MESH)
            return carry

        lax.fori_loop(1, n, step, 0)

    greet(G, g, plane)
    greet(Z, f, along_z)

    ex_part = Exchange(G, g, plane, lambda j: part.at[j], lambda i: part_r.at[i], s_tp.at[0], r_tp.at[0])
    ex_proj = Exchange(G, g, plane, lambda j: proj.at[g], lambda i: proj.at[i], s_tp.at[1], r_tp.at[1])
    ex_gram = Exchange(Z, f, along_z, lambda j: gram_p.at[j], lambda i: gram_r.at[i], s_z.at[0], r_z.at[0])
    ex_gall = Exchange(Z, f, along_z, lambda j: gram.at[f], lambda i: gram.at[i], s_z.at[1], r_z.at[1])
    ex_a1 = Exchange(Z, f, along_z, lambda j: wa.at[j], lambda i: ra1.at[i], s_z.at[2], r_z.at[2])
    ex_b1 = Exchange(Y, r, along_y, lambda j: wb.at[j], lambda i: rb1.at[i], s_y.at[0], r_y.at[0])
    ex_a2 = Exchange(Y, r, along_y, lambda j: sa1.at[j], lambda i: ra2.at[i], s_y.at[1], r_y.at[1])
    ex_b2 = Exchange(Z, f, along_z, lambda j: sb1.at[j], lambda i: rb2.at[i], s_z.at[3], r_z.at[3])
    ga1 = Exchange(Y, r, along_y, lambda j: rta.at[f, r], lambda i: rta.at[f, i], s_y.at[2], r_y.at[2])
    gb1 = Exchange(Z, f, along_z, lambda j: rtb.at[r, f], lambda i: rtb.at[r, i], s_z.at[4], r_z.at[4])
    ga2 = Exchange(Z, f, along_z, lambda j: rta.at[f], lambda i: rta.at[i], s_z.at[5], r_z.at[5])
    gb2 = Exchange(Y, r, along_y, lambda j: rtb.at[r], lambda i: rtb.at[i], s_y.at[3], r_y.at[3])
    ex_qt = Exchange(T, t, along_t, lambda j: sq_t.at[t], lambda i: sq_t.at[i], s_z.at[6], r_z.at[6])
    ex_qy = Exchange(Y, r, along_y, lambda j: sq_y.at[r], lambda i: sq_y.at[i], s_y.at[4], r_y.at[4])
    ex_qz = Exchange(Z, f, along_z, lambda j: sq_z.at[f], lambda i: sq_z.at[i], s_z.at[7], r_z.at[7])

    loads[0].wait()
    q_h, q_l = split(q_v[...])
    q_hl[:, 0:128] = q_h
    q_hl[:, 128:256] = q_l
    acc = None
    for c in range(4):
        cols = pl.ds(512 * c, 512)
        loads[2 * c + 1].wait()
        loads[2 * c + 2].wait()
        b_h, b_l = split(mom_v[:, cols] + grad_v[:, cols].astype(F32))
        hi_v[:, cols] = b_h
        lo_v[:, cols] = b_l
        both = mm(b_h, q_hl[cols, :])
        term = both[:, 0:128] + (both[:, 128:256] + mm(b_l, q_hl[cols, 0:128]))
        acc = term if acc is None else acc + term
    part[...] = acc.reshape(G, 16, 128)
    part_r[pl.ds(g, 1)] = part[pl.ds(g, 1)]

    pl.semaphore_wait(barrier, G + Z - 2)
    ex_part.start()
    ex_part.wait_recv()
    proj[pl.ds(g, 1)] = total(part_r, G)[None]
    ex_proj.start()
    ex_proj.wait_recv()

    p = proj[...].reshape(512, 128)
    pt = p.T
    pt_h, pt_l = split(pt)
    gram_p[...] = mmf(pt, p).reshape(Z, 16, 128)
    gram_r[pl.ds(f, 1)] = gram_p[pl.ds(f, 1)]
    ex_gram.start()

    def columns(lo, n):
        b_h = hi_v[:, lo : lo + n]
        w = mm(pt_h, b_h) + (mm(pt_l, b_h) + mm(pt_h, lo_v[:, lo : lo + n]))
        return w.T

    for c in range(2):
        wa[4 * c : 4 * c + 4] = columns(512 * c, 512).reshape(4, 128, 128)
    ra1[pl.ds(f, 1)] = wa[pl.ds(f, 1)]
    ex_a1.start()
    for c in range(2):
        wb[2 * c : 2 * c + 2] = columns(1024 + 512 * c, 512).reshape(2, 256, 128)
    rb1[pl.ds(r, 1)] = wb[pl.ds(r, 1)]
    ex_b1.start()

    ex_gram.wait_recv()
    gram[pl.ds(f, 1)] = total(gram_r, Z)[None]
    ex_gall.start()

    ex_b1.wait_recv()
    sb1[...] = total(rb1, Y).reshape(Z, 32, 128)
    rb2[pl.ds(f, 1)] = sb1[pl.ds(f, 1)]
    ex_b2.start()
    ex_a1.wait_recv()
    sa1[...] = total(ra1, Z).reshape(Y, 32, 128)
    ra2[pl.ds(r, 1)] = sa1[pl.ds(r, 1)]
    ex_a2.start()

    ex_gall.wait_recv()
    inverse = factor(work, gram[...].reshape(128, 128))

    ex_a2.wait_recv()
    ex_b2.wait_recv()
    w = jnp.concatenate([total(ra2, Y), total(rb2, Z)], axis=0)
    right = 0.25 * mmf(w, inverse, ((1,), (1,)))
    rta[pl.ds(f, 1), pl.ds(r, 1)] = right[0:32][None, None]
    rtb[pl.ds(r, 1), pl.ds(f, 1)] = right[32:64][None, None]
    ga1.start()
    gb1.start()
    squares = jnp.sum(right * right, axis=0, keepdims=True)
    sq_t[pl.ds(t, 1)] = jnp.broadcast_to(squares, (8, 128))[None]
    ex_qt.start()
    basis_v[...] = mmf(p, inverse, ((1,), (1,)))
    keep_basis = pltpu.make_async_copy(basis_v, basis_out, store.at[0])
    keep_basis.start()

    ex_qt.wait_recv()
    sq_y[pl.ds(r, 1)] = total(sq_t, T)[None]
    ex_qy.start()
    ga1.wait_recv()
    ga2.start()
    ex_qy.wait_recv()
    sq_z[pl.ds(f, 1)] = total(sq_y, Y)[None]
    ex_qz.start()
    gb1.wait_recv()
    gb2.start()
    ex_qz.wait_recv()
    sq_out[...] = total(sq_z, Z)
    gb2.wait_recv()
    keep_b = pltpu.make_async_copy(rtb, right_out.at[1], store.at[1])
    keep_a = pltpu.make_async_copy(rta.reshape(Y, Z, 32, 128), right_out.at[0], store.at[2])
    keep_b.start()
    ga2.wait_recv()
    keep_a.start()
    for ex in (ex_part, ex_proj, ex_gram, ex_gall, ex_a1, ex_b1, ex_a2, ex_b2, ga1, gb1, ga2, gb2, ex_qt, ex_qy, ex_qz):
        ex.wait_send()
    keep_basis.wait()
    keep_b.wait()
    keep_a.wait()


def finish(mom, grad, weight, right, basis, sq, weight_out, mom_out, q_out):
    r = right[...]
    scale = lax.rsqrt(sq[0:1] * (1.0 / 16384.0) + 1e-06)
    q_out[...] = r * scale
    r_h, r_l = split(r)
    nt = ((1,), (1,))
    b = basis[...]
    b_h, b_l = split(b)
    feedback = mm(b_h, r_h, nt) + (mm(b_h, r_l, nt) + mm(b_l, r_h, nt))
    mom_out[...] = (mom[...] + grad[...].astype(F32)) - 0.05 * feedback
    s_h, s_l = split(b * scale)
    update = mm(s_h, r_h, nt) + (mm(s_h, r_l, nt) + mm(s_l, r_h, nt))
    weight_out[...] = 0.999 * weight[...] - 0.2 * update


def shards(weight, momentum, gradient, q_in):
    mom, grad = momentum[0], gradient[0]
    vm = lambda *shape: pltpu.VMEM(shape, F32)
    dma = lambda *shape: pltpu.SemaphoreType.DMA(shape)
    any_ = pl.BlockSpec(memory_space=pl.ANY)
    right, basis, sq = pl.pallas_call(
        talk,
        out_shape=(
            jax.ShapeDtypeStruct((2, Y, Z, 32, 128), F32),
            jax.ShapeDtypeStruct((512, 128), F32),
            jax.ShapeDtypeStruct((8, 128), F32),
        ),
        in_specs=[any_] * 3,
        out_specs=(any_, any_, pl.BlockSpec(memory_space=pltpu.VMEM)),
        scratch_shapes=[
            vm(512, 2048), pltpu.VMEM((512, 2048), BF16), vm(2048, 128),
            pltpu.VMEM((512, 2048), BF16), pltpu.VMEM((512, 2048), BF16), pltpu.VMEM((2048, 256), BF16),
            vm(G, 16, 128), vm(G, 16, 128), vm(G, 16, 128),
            vm(Z, 16, 128), vm(Z, 16, 128), vm(Z, 16, 128),
            vm(Z, 128, 128), vm(Y, 256, 128), vm(Z, 128, 128), vm(Y, 256, 128),
            vm(Y, 32, 128), vm(Z, 32, 128), vm(Y, 32, 128), vm(Z, 32, 128),
            vm(Z, Y, 32, 128), vm(Y, Z, 32, 128),
            vm(128, 256), vm(512, 128), vm(T, 8, 128), vm(Y, 8, 128), vm(Z, 8, 128),
            dma(9), dma(3), dma(2, G), dma(2, G), dma(8, Z), dma(8, Z), dma(5, Y), dma(5, Y),
        ],
        compiler_params=pltpu.CompilerParams(collective_id=0, has_side_effects=True, vmem_limit_bytes=28 << 20),
        cost_estimate=pl.CostEstimate(flops=1 << 31, bytes_accessed=8 << 20, transcendentals=0),
    )(mom, grad, q_in)
    right = right.reshape(2048, 128)
    n = 512
    wide = pl.BlockSpec((512, n), lambda i: (0, i))
    tall = pl.BlockSpec((n, 128), lambda i: (i, 0))
    whole = lambda rows: pl.BlockSpec((rows, 128), lambda i: (0, 0))
    weight_new, momentum_new, q_new = pl.pallas_call(
        finish,
        grid=(2048 // n,),
        out_shape=(
            jax.ShapeDtypeStruct((512, 2048), F32),
            jax.ShapeDtypeStruct((512, 2048), F32),
            jax.ShapeDtypeStruct((2048, 128), F32),
        ),
        in_specs=[wide, wide, wide, tall, whole(512), whole(8)],
        out_specs=(wide, wide, tall),
        compiler_params=pltpu.CompilerParams(vmem_limit_bytes=24 << 20),
        cost_estimate=pl.CostEstimate(flops=1 << 31, bytes_accessed=21 << 20, transcendentals=0),
    )(mom, grad, weight, right, basis, sq)
    return (weight_new, momentum_new[None], q_new)


def solution(mesh):
    placed = (P("fsdp", "tp"), P("rep", "fsdp", "tp"), P("rep", "fsdp", "tp"), P("tp", None))
    return jax.shard_map(
        shards,
        mesh=mesh,
        in_specs=placed,
        out_specs=(P("fsdp", "tp"), P("rep", "fsdp", "tp"), P("tp", None)),
        check_vma=False,
    )
```

time: 423 us -> 93.9 us (0.22)
  waiting for transfers between devices: 333 us -> 0 us
  Pallas kernels: 0 us -> 84.9 us
  matrix products: 32.6 us -> 0 us
  other arithmetic: 26.5 us -> 0 us
  between operations: 13.8 us -> 0.67 us
  blocking collectives: 12.4 us -> 0 us
  local copies, waits for them, and re-layouts: 2.11 us -> 7.18 us
    psum x3 -> x0, waiting for transfers between devices: 333 us -> none  [the longest x1 147 us: shards(): right = lax.psum(transposed(buffer, basis), ('fsdp', 'rep')) / replicas]
    pallas_call x0 -> x2, Pallas kernels: none -> 84.9 us  [the longest x1 79.1 us: shards(): pl.pallas_call(talk, out_shape=(jax.ShapeDtypeStruct((2, Y, Z, 32, 128),...]
    dot_general x5 -> x0, matrix products: 31.3 us -> none  [the longest x1 10.1 us: transposed(): lax.dot_general(block, basis, (((0,), (0,)), ((), ())), precision=lax.Pre...]
    another operation x5 -> x0, other arithmetic: 22.9 us -> none  [the longest x3 12.4 us: shards(): lower = jnp.linalg.cholesky(gram)]
    psum x1 -> x0, blocking collectives: 12.4 us -> none  [shards(): squares = lax.psum(jnp.sum(right * right, axis=0), 'tp')]
    unnamed x10, local copies, waits for them, and re-layouts: 1.19 us -> 7.18 us
  transfers between devices with their start and end apart: 3 -> 0, of which waited for: 3 -> 0; matrix products, arithmetic and copies ran while one was open for 0% -> 0% of each run, Pallas kernels for 0% -> 0%
where the time goes in v1:
time: 93.9 us; the launch traced here: 92.8 us
  Pallas kernels  84.9 us (90%)
  local copies, waits for them, and re-layouts  7.18 us (8%)
    pallas_call x1, Pallas kernels, shards(): pl.pallas_call(talk, out_shape=(jax.ShapeDtypeStruct((2, Y, Z, 32, 128),...  79.1 us
    unnamed x10, local copies, waits for them, and re-layouts  7.18 us
    pallas_call x1, Pallas kernels, shards(): pl.pallas_call(finish, grid=(2048 // n,), out_shape=(jax.ShapeDtypeStruct...  5.8 us

profile of v1, /device:TPU:32, one launch (start us, length us, event | category | flops | bytes accessed | tf_op | source)
XLA Modules:
  0.0 92.8 jit_solution(17384499268322374487)
XLA Ops:
  0.6 0.0 copy-start
  0.6 2.2 %copy-done = f32[1,512,2048]{2,1,0:T(8,128)S(1)} copy-done((f32[1,512,2048]{2,1,0:T(8,128)S(1)}, f32[1,512,2048]{2,1,0:T(8,128)}, u32[]{:S(2)}) %copy-start) | copy-done | bytes 4194328
  2.8 0.0 copy-start.3
  2.8 1.6 %copy-done.3 = bf16[1,512,2048]{2,1,0:T(8,128)(2,1)S(1)} copy-done((bf16[1,512,2048]{2,1,0:T(8,128)(2,1)S(1)}, bf16[1,512,2048]{2,1,0:T(8,128)(2,1)}, u32[]{:S(2)}) %copy-start.3) | copy-done | bytes 2097176
  4.4 0.0 copy-start.4
  4.4 1.2 %copy-done.4 = f32[2048,128]{1,0:T(8,128)S(1)} copy-done((f32[2048,128]{1,0:T(8,128)S(1)}, f32[2048,128]{1,0:T(8,128)}, u32[]{:S(2)}) %copy-start.4) | copy-done | bytes 1048600
  5.6 0.0 copy-start.1
  5.6 79.1 %shard_map.67 = (f32[2,4,8,32,128]{4,3,2,1,0:T(8,128)S(1)}, f32[512,128]{1,0:T(8,128)S(1)}, f32[8,128]{1,0:T(8,128)S(1)}) custom-call(f32[512,2048]{1,0:T(8,128)S(1)} %bitcast.4, bf16[512,2048]{1,0:T(8,128)(2,1)S(1)} %bitcast.6, f32[2048,128]{1,0:T(8,128)S(1)} %copy-done.4), custom_call_target="tpu_custom_call" | custom-call | flops 2147483648 | bytes 8388608 | tf_op jit(solution)/shard_map/pallas_call | solution.py:261
  84.8 0.0 copy-done.1
  84.8 0.0 copy-start.2
  84.8 2.2 %copy-done.2 = f32[512,2048]{1,0:T(8,128)S(1)} copy-done((f32[512,2048]{1,0:T(8,128)S(1)}, f32[512,2048]{1,0:T(8,128)}, u32[]{:S(2)}) %copy-start.2) | copy-done | bytes 4194328
  87.0 5.8 %shard_map.68 = (f32[512,2048]{1,0:T(8,128)}, f32[512,2048]{1,0:T(8,128)}, f32[2048,128]{1,0:T(8,128)}) custom-call(f32[512,2048]{1,0:T(8,128)S(1)} %bitcast.5, bf16[512,2048]{1,0:T(8,128)(2,1)S(1)} %bitcast.7, f32[512,2048]{1,0:T(8,128)S(1)} %copy-done.2, f32[2048,128]{1,0:T(8,128)S(1)} %bitcast.8, f32[512,128]{1,0:T(8,128)S(1)} %get-tuple-element.10.basis, ...), custom_call_target="tpu_custom_call" | custom-call | flops 2147483648 | bytes 22020096 | tf_op jit(solution)/shard_map/pallas_call | solution.py:289
Async XLA Ops:
  0.6 2.2 %copy-start = (f32[1,512,2048]{2,1,0:T(8,128)S(1)}, f32[1,512,2048]{2,1,0:T(8,128)}, u32[]{:S(2)}) copy-start(f32[1,512,2048]{2,1,0:T(8,128)} %param.5) | copy-start | bytes 12582916
  2.8 1.6 %copy-start.3 = (bf16[1,512,2048]{2,1,0:T(8,128)(2,1)S(1)}, bf16[1,512,2048]{2,1,0:T(8,128)(2,1)}, u32[]{:S(2)}) copy-start(bf16[1,512,2048]{2,1,0:T(8,128)(2,1)} %param.6) | copy-start | bytes 6291460
  4.4 1.2 %copy-start.4 = (f32[2048,128]{1,0:T(8,128)S(1)}, f32[2048,128]{1,0:T(8,128)}, u32[]{:S(2)}) copy-start(f32[2048,128]{1,0:T(8,128)} %q_in.1) | copy-start | bytes 3145732
  5.6 79.1 %copy-start.1 = (f32[1,512,2048]{2,1,0:T(8,128)S(1)}, f32[1,512,2048]{2,1,0:T(8,128)}, u32[]{:S(2)}) copy-start(f32[1,512,2048]{2,1,0:T(8,128)} %param.5) | copy-start | bytes 12582916
  84.8 2.2 %copy-start.2 = (f32[512,2048]{1,0:T(8,128)S(1)}, f32[512,2048]{1,0:T(8,128)}, u32[]{:S(2)}) copy-start(f32[512,2048]{1,0:T(8,128)} %weight.1) | copy-start | bytes 12582916

commit v2 on v1

--- a/solution.py
+++ b/solution.py
@@ -67,25 +67,45 @@
 def factor(work, gram):
     rows = lax.broadcasted_iota(jnp.int32, (128, 128), 0)
     lanes = lax.broadcasted_iota(jnp.int32, (128, 128), 1)
+    lane = lanes[0:1]
     work[:, 0:128] = gram
     work[:, 128:256] = jnp.where(rows == lanes, 1.0, 0.0).astype(F32)
-
-    def pivot(j, carry):
-        row = work[pl.ds(j, 1), :]
-        left = work[:, 0:128]
-        col = jnp.sum(jnp.where(lanes == j, left, 0.0), axis=1, keepdims=True)
-        d = jnp.sum(jnp.where(lanes[0:1] == j, row[:, 0:128], 0.0), axis=1, keepdims=True)
-        m = jnp.where(rows[:, 0:1] > j, col * (1.0 / d), 0.0)
-        work[...] = work[...] - m * row
-        return carry
-
-    lax.fori_loop(0, 128, pivot, 0)
+    for low in range(0, 128, 32):
+        below = lax.broadcasted_iota(jnp.int32, (128 - low, 1), 0) + low
+        wide = lanes[low:128]
+
+        def step(k, carry):
+            j = 4 * k
+            row = [work[pl.ds(j + s, 1), :] for s in range(4)]
+            left = work[low:128, 0:128]
+            col = [jnp.sum(jnp.where(wide == j + s, left, 0.0), axis=1, keepdims=True) for s in range(4)]
+            e = {}
+            for a in range(4):
+                for b in range(a, 4):
+                    e[a, b] = jnp.sum(jnp.where(lane == j + b, row[a][:, 0:128], 0.0), axis=1, keepdims=True)
+            update = None
+            for a in range(4):
+                inv = 1.0 / e[a, a]
+                for b in range(a + 1, 4):
+                    q = e[a, b] * inv
+                    row[b] = row[b] - q * row[a]
+                    for c in range(b, 4):
+                        e[b, c] = e[b, c] - q * e[a, c]
+                    col[b] = col[b] - q * col[a]
+                term = jnp.where(below > j + 3, col[a] * inv, 0.0) * row[a]
+                update = term if update is None else update + term
+            work[low:128, :] = work[low:128, :] - update
+            for a in range(1, 4):
+                work[pl.ds(j + a, 1), :] = row[a]
+            return carry
+
+        lax.fori_loop(low // 4, low // 4 + 8, step, 0)
     d = jnp.sum(jnp.where(rows == lanes, work[:, 0:128], 0.0), axis=1, keepdims=True)
     return work[:, 128:256] * lax.rsqrt(d)
 
 
 def talk(
-    mom, grad, q_in, right_out, basis_out, sq_out,
+    mom, grad, q_in, weight, right_out, basis_out, sq_out, buffer_out, weight_out,
     mom_v, grad_v, q_v, hi_v, lo_v, q_hl,
     part, part_r, proj, gram_p, gram_r, gram,
     wa, wb, ra1, rb1, sa1, sb1, ra2, rb2, rta, rtb,
@@ -102,6 +122,7 @@
         loads.append(pltpu.make_async_copy(grad.at[:, cols], grad_v.at[:, cols], load.at[2 * c + 1]))
     for cp in loads:
         cp.start()
+    keep_weight = pltpu.make_async_copy(weight, weight_out, load.at[9])
 
     plane = lambda j: {"tp": lax.div(j, Y), "rep": lax.rem(j, Y)}
     along_z = lambda j: {"fsdp": j}
@@ -145,7 +166,9 @@
         cols = pl.ds(512 * c, 512)
         loads[2 * c + 1].wait()
         loads[2 * c + 2].wait()
-        b_h, b_l = split(mom_v[:, cols] + grad_v[:, cols].astype(F32))
+        b = mom_v[:, cols] + grad_v[:, cols].astype(F32)
+        mom_v[:, cols] = b
+        b_h, b_l = split(b)
         hi_v[:, cols] = b_h
         lo_v[:, cols] = b_l
         both = mm(b_h, q_hl[cols, :])
@@ -155,6 +178,9 @@
     part_r[pl.ds(g, 1)] = part[pl.ds(g, 1)]
 
     pl.semaphore_wait(barrier, G + Z - 2)
+    keep_weight.start()
+    keep_buffer = pltpu.make_async_copy(mom_v, buffer_out, load.at[10])
+    keep_buffer.start()
     ex_part.start()
     ex_part.wait_recv()
     proj[pl.ds(g, 1)] = total(part_r, G)[None]
@@ -174,44 +200,41 @@
         return w.T
 
     for c in range(2):
-        wa[4 * c : 4 * c + 4] = columns(512 * c, 512).reshape(4, 128, 128)
+        wa[4 * c : 4 * c + 4] = columns(384 * c, 384).reshape(4, 96, 128)
     ra1[pl.ds(f, 1)] = wa[pl.ds(f, 1)]
     ex_a1.start()
     for c in range(2):
-        wb[2 * c : 2 * c + 2] = columns(1024 + 512 * c, 512).reshape(2, 256, 128)
+        wb[2 * c : 2 * c + 2] = columns(768 + 640 * c, 640).reshape(2, 320, 128)
     rb1[pl.ds(r, 1)] = wb[pl.ds(r, 1)]
     ex_b1.start()
 
     ex_gram.wait_recv()
     gram[pl.ds(f, 1)] = total(gram_r, Z)[None]
     ex_gall.start()
-
     ex_b1.wait_recv()
-    sb1[...] = total(rb1, Y).reshape(Z, 32, 128)
+    sb1[...] = total(rb1, Y).reshape(Z, 40, 128)
     rb2[pl.ds(f, 1)] = sb1[pl.ds(f, 1)]
     ex_b2.start()
+    ex_gall.wait_recv()
+    inverse = factor(work, gram[...].reshape(128, 128))
     ex_a1.wait_recv()
-    sa1[...] = total(ra1, Z).reshape(Y, 32, 128)
+    sa1[...] = total(ra1, Z).reshape(Y, 24, 128)
     ra2[pl.ds(r, 1)] = sa1[pl.ds(r, 1)]
     ex_a2.start()
-
-    ex_gall.wait_recv()
-    inverse = factor(work, gram[...].reshape(128, 128))
-
+    basis_v[...] = mmf(p, inverse, ((1,), (1,)))
+    keep_basis = pltpu.make_async_copy(basis_v, basis_out, store.at[0])
+    keep_basis.start()
     ex_a2.wait_recv()
     ex_b2.wait_recv()
     w = jnp.concatenate([total(ra2, Y), total(rb2, Z)], axis=0)
     right = 0.25 * mmf(w, inverse, ((1,), (1,)))
-    rta[pl.ds(f, 1), pl.ds(r, 1)] = right[0:32][None, None]
-    rtb[pl.ds(r, 1), pl.ds(f, 1)] = right[32:64][None, None]
+    rta[pl.ds(f, 1), pl.ds(r, 1)] = right[0:24][None, None]
+    rtb[pl.ds(r, 1), pl.ds(f, 1)] = right[24:64][None, None]
     ga1.start()
     gb1.start()
     squares = jnp.sum(right * right, axis=0, keepdims=True)
     sq_t[pl.ds(t, 1)] = jnp.broadcast_to(squares, (8, 128))[None]
     ex_qt.start()
-    basis_v[...] = mmf(p, inverse, ((1,), (1,)))
-    keep_basis = pltpu.make_async_copy(basis_v, basis_out, store.at[0])
-    keep_basis.start()
 
     ex_qt.wait_recv()
     sq_y[pl.ds(r, 1)] = total(sq_t, T)[None]
@@ -226,19 +249,21 @@
     ex_qz.wait_recv()
     sq_out[...] = total(sq_z, Z)
     gb2.wait_recv()
-    keep_b = pltpu.make_async_copy(rtb, right_out.at[1], store.at[1])
-    keep_a = pltpu.make_async_copy(rta.reshape(Y, Z, 32, 128), right_out.at[0], store.at[2])
+    keep_b = pltpu.make_async_copy(rtb.reshape(1280, 128), right_out.at[768:2048], store.at[1])
+    keep_a = pltpu.make_async_copy(rta.reshape(768, 128), right_out.at[0:768], store.at[2])
     keep_b.start()
     ga2.wait_recv()
     keep_a.start()
     for ex in (ex_part, ex_proj, ex_gram, ex_gall, ex_a1, ex_b1, ex_a2, ex_b2, ga1, gb1, ga2, gb2, ex_qt, ex_qy, ex_qz):
         ex.wait_send()
+    keep_weight.wait()
+    keep_buffer.wait()
     keep_basis.wait()
     keep_b.wait()
     keep_a.wait()
 
 
-def finish(mom, grad, weight, right, basis, sq, weight_out, mom_out, q_out):
+def finish(buffer, weight, right, basis, sq, weight_out, mom_out, q_out):
     r = right[...]
     scale = lax.rsqrt(sq[0:1] * (1.0 / 16384.0) + 1e-06)
     q_out[...] = r * scale
@@ -247,7 +272,7 @@
     b = basis[...]
     b_h, b_l = split(b)
     feedback = mm(b_h, r_h, nt) + (mm(b_h, r_l, nt) + mm(b_l, r_h, nt))
-    mom_out[...] = (mom[...] + grad[...].astype(F32)) - 0.05 * feedback
+    mom_out[...] = buffer[...] - 0.05 * feedback
     s_h, s_l = split(b * scale)
     update = mm(s_h, r_h, nt) + (mm(s_h, r_l, nt) + mm(s_l, r_h, nt))
     weight_out[...] = 0.999 * weight[...] - 0.2 * update
@@ -258,30 +283,32 @@
     vm = lambda *shape: pltpu.VMEM(shape, F32)
     dma = lambda *shape: pltpu.SemaphoreType.DMA(shape)
     any_ = pl.BlockSpec(memory_space=pl.ANY)
-    right, basis, sq = pl.pallas_call(
+    hbm = pl.BlockSpec(memory_space=pltpu.HBM)
+    right, basis, sq, buffer, weight = pl.pallas_call(
         talk,
         out_shape=(
-            jax.ShapeDtypeStruct((2, Y, Z, 32, 128), F32),
+            jax.ShapeDtypeStruct((2048, 128), F32),
             jax.ShapeDtypeStruct((512, 128), F32),
             jax.ShapeDtypeStruct((8, 128), F32),
+            pltpu.VMEM((512, 2048), F32),
+            pltpu.VMEM((512, 2048), F32),
         ),
-        in_specs=[any_] * 3,
-        out_specs=(any_, any_, pl.BlockSpec(memory_space=pltpu.VMEM)),
+        in_specs=[hbm] * 4,
+        out_specs=(any_, any_, pl.BlockSpec(memory_space=pltpu.VMEM), any_, any_),
         scratch_shapes=[
             vm(512, 2048), pltpu.VMEM((512, 2048), BF16), vm(2048, 128),
             pltpu.VMEM((512, 2048), BF16), pltpu.VMEM((512, 2048), BF16), pltpu.VMEM((2048, 256), BF16),
             vm(G, 16, 128), vm(G, 16, 128), vm(G, 16, 128),
             vm(Z, 16, 128), vm(Z, 16, 128), vm(Z, 16, 128),
-            vm(Z, 128, 128), vm(Y, 256, 128), vm(Z, 128, 128), vm(Y, 256, 128),
-            vm(Y, 32, 128), vm(Z, 32, 128), vm(Y, 32, 128), vm(Z, 32, 128),
-            vm(Z, Y, 32, 128), vm(Y, Z, 32, 128),
+            vm(Z, 96, 128), vm(Y, 320, 128), vm(Z, 96, 128), vm(Y, 320, 128),
+            vm(Y, 24, 128), vm(Z, 40, 128), vm(Y, 24, 128), vm(Z, 40, 128),
+            vm(Z, Y, 24, 128), vm(Y, Z, 40, 128),
             vm(128, 256), vm(512, 128), vm(T, 8, 128), vm(Y, 8, 128), vm(Z, 8, 128),
-            dma(9), dma(3), dma(2, G), dma(2, G), dma(8, Z), dma(8, Z), dma(5, Y), dma(5, Y),
+            dma(11), dma(3), dma(2, G), dma(2, G), dma(8, Z), dma(8, Z), dma(5, Y), dma(5, Y),
         ],
         compiler_params=pltpu.CompilerParams(collective_id=0, has_side_effects=True, vmem_limit_bytes=28 << 20),
         cost_estimate=pl.CostEstimate(flops=1 << 31, bytes_accessed=8 << 20, transcendentals=0),
-    )(mom, grad, q_in)
-    right = right.reshape(2048, 128)
+    )(*(pltpu.with_memory_space_constraint(x, pltpu.HBM) for x in (mom, grad, q_in, weight)))
     n = 512
     wide = pl.BlockSpec((512, n), lambda i: (0, i))
     tall = pl.BlockSpec((n, 128), lambda i: (i, 0))
@@ -294,11 +321,11 @@
             jax.ShapeDtypeStruct((512, 2048), F32),
             jax.ShapeDtypeStruct((2048, 128), F32),
         ),
-        in_specs=[wide, wide, wide, tall, whole(512), whole(8)],
+        in_specs=[wide, wide, tall, whole(512), whole(8)],
         out_specs=(wide, wide, tall),
         compiler_params=pltpu.CompilerParams(vmem_limit_bytes=24 << 20),
         cost_estimate=pl.CostEstimate(flops=1 << 31, bytes_accessed=21 << 20, transcendentals=0),
-    )(mom, grad, weight, right, basis, sq)
+    )(buffer, weight, right, basis, sq)
     return (weight_new, momentum_new[None], q_new)
 
 

time: 93.9 us -> 76 us (0.81)
  Pallas kernels: 84.9 us -> 74.3 us
  local copies, waits for them, and re-layouts: 7.18 us -> 0 us
    pallas_call x1, Pallas kernels: 79.1 us -> 68.6 us  [shards(): pl.pallas_call(talk, out_shape=(jax.ShapeDtypeStruct((2048, 128), F32), j...]
    unnamed x10 -> x0, local copies, waits for them, and re-layouts: 7.18 us -> none
where the time goes in v2:
time: 76 us; the launch traced here: 74.9 us
  Pallas kernels  74.3 us (98%)
    pallas_call x1, Pallas kernels, shards(): pl.pallas_call(talk, out_shape=(jax.ShapeDtypeStruct((2048, 128), F32), j...  68.6 us
    pallas_call x1, Pallas kernels, shards(): pl.pallas_call(finish, grid=(2048 // n,), out_shape=(jax.ShapeDtypeStruct...  5.65 us

profile of v2, /device:TPU:32, one launch (start us, length us, event | category | flops | bytes accessed | tf_op | source)
XLA Modules:
  0.0 74.9 jit_solution(3099207420575774515)
XLA Ops:
  0.6 68.6 %shard_map.67 = (f32[2048,128]{1,0:T(8,128)S(1)}, f32[512,128]{1,0:T(8,128)S(1)}, f32[8,128]{1,0:T(8,128)S(1)}, f32[512,2048]{1,0:T(8,128)S(1)}, f32[512,2048]{1,0:T(8,128)S(1)}) custom-call(f32[512,2048]{1,0:T(8,128)} %bitcast.3, bf16[512,2048]{1,0:T(8,128)(2,1)} %bitcast.4, f32[2048,128]{1,0:T(8,128)} %q_in.1, f32[512,2048]{1,0:T(8,128)} %weight.1), custom_call_target="tpu_custom_call" | custom-call | flops 2147483648 | bytes 8388608 | tf_op jit(solution)/shard_map/pallas_call | solution.py:287
  69.3 5.6 %shard_map.68 = (f32[512,2048]{1,0:T(8,128)}, f32[512,2048]{1,0:T(8,128)}, f32[2048,128]{1,0:T(8,128)}) custom-call(f32[512,2048]{1,0:T(8,128)S(1)} %get-tuple-element.11.buffer, f32[512,2048]{1,0:T(8,128)S(1)} %get-tuple-element.12.weight, f32[2048,128]{1,0:T(8,128)S(1)} %get-tuple-element.13.right, f32[512,128]{1,0:T(8,128)S(1)} %get-tuple-element.14.basis, ...), custom_call_target="tpu_custom_call" | custom-call | flops 2147483648 | bytes 22020096 | tf_op jit(solution)/shard_map/pallas_call | solution.py:316

commit v3 on v2

--- a/solution.py
+++ b/solution.py
@@ -46,6 +46,12 @@
             device_id=self.device(j),
             device_id_type=MESH,
         )
+
+    def start_one(self, j):
+        self.copy(j, self.me).start()
+
+    def recv_one(self, j):
+        self.copy(j, j).wait_recv()
 
     def start(self):
         self.each(lambda j: self.copy(j, self.me).start())
@@ -100,6 +106,12 @@
             return carry
 
         lax.fori_loop(low // 4, low // 4 + 8, step, 0)
+        yield
+
+
+def inverse_factor(work):
+    rows = lax.broadcasted_iota(jnp.int32, (128, 128), 0)
+    lanes = lax.broadcasted_iota(jnp.int32, (128, 128), 1)
     d = jnp.sum(jnp.where(rows == lanes, work[:, 0:128], 0.0), axis=1, keepdims=True)
     return work[:, 128:256] * lax.rsqrt(d)
 
@@ -110,7 +122,7 @@
     part, part_r, proj, gram_p, gram_r, gram,
     wa, wb, ra1, rb1, sa1, sb1, ra2, rb2, rta, rtb,
     work, basis_v, sq_t, sq_y, sq_z,
-    load, store, s_tp, r_tp, s_z, r_z, s_y, r_y,
+    load, store, s_tp, r_tp, s_z, r_z, s_y, r_y, s_pa, r_pa, s_pb, r_pb,
 ):
     f, t, r = lax.axis_index("fsdp"), lax.axis_index("tp"), lax.axis_index("rep")
     g = t * Y + r
@@ -145,17 +157,27 @@
     ex_proj = Exchange(G, g, plane, lambda j: proj.at[g], lambda i: proj.at[i], s_tp.at[1], r_tp.at[1])
     ex_gram = Exchange(Z, f, along_z, lambda j: gram_p.at[j], lambda i: gram_r.at[i], s_z.at[0], r_z.at[0])
     ex_gall = Exchange(Z, f, along_z, lambda j: gram.at[f], lambda i: gram.at[i], s_z.at[1], r_z.at[1])
-    ex_a1 = Exchange(Z, f, along_z, lambda j: wa.at[j], lambda i: ra1.at[i], s_z.at[2], r_z.at[2])
-    ex_b1 = Exchange(Y, r, along_y, lambda j: wb.at[j], lambda i: rb1.at[i], s_y.at[0], r_y.at[0])
-    ex_a2 = Exchange(Y, r, along_y, lambda j: sa1.at[j], lambda i: ra2.at[i], s_y.at[1], r_y.at[1])
-    ex_b2 = Exchange(Z, f, along_z, lambda j: sb1.at[j], lambda i: rb2.at[i], s_z.at[3], r_z.at[3])
-    ga1 = Exchange(Y, r, along_y, lambda j: rta.at[f, r], lambda i: rta.at[f, i], s_y.at[2], r_y.at[2])
-    gb1 = Exchange(Z, f, along_z, lambda j: rtb.at[r, f], lambda i: rtb.at[r, i], s_z.at[4], r_z.at[4])
-    ga2 = Exchange(Z, f, along_z, lambda j: rta.at[f], lambda i: rta.at[i], s_z.at[5], r_z.at[5])
-    gb2 = Exchange(Y, r, along_y, lambda j: rtb.at[r], lambda i: rtb.at[i], s_y.at[3], r_y.at[3])
-    ex_qt = Exchange(T, t, along_t, lambda j: sq_t.at[t], lambda i: sq_t.at[i], s_z.at[6], r_z.at[6])
-    ex_qy = Exchange(Y, r, along_y, lambda j: sq_y.at[r], lambda i: sq_y.at[i], s_y.at[4], r_y.at[4])
-    ex_qz = Exchange(Z, f, along_z, lambda j: sq_z.at[f], lambda i: sq_z.at[i], s_z.at[7], r_z.at[7])
+    ex_a2 = Exchange(Y, r, along_y, lambda j: sa1.at[j], lambda i: ra2.at[i], s_y.at[0], r_y.at[0])
+    ex_b2 = Exchange(Z, f, along_z, lambda j: sb1.at[j], lambda i: rb2.at[i], s_z.at[2], r_z.at[2])
+
+    def ex_a1(p):
+        return Exchange(Z, f, along_z, lambda j: wa.at[j, p], lambda i: ra1.at[i, p], s_pa.at[0, p], r_pa.at[0, p])
+
+    def ex_b1(p):
+        return Exchange(Y, r, along_y, lambda j: wb.at[j, p], lambda i: rb1.at[i, p], s_pb.at[0, p], r_pb.at[0, p])
+
+    ga1 = Exchange(Y, r, along_y, lambda j: rta.at[f, r], lambda i: rta.at[f, i], s_y.at[1], r_y.at[1])
+    gb1 = Exchange(Z, f, along_z, lambda j: rtb.at[r, f], lambda i: rtb.at[r, i], s_z.at[3], r_z.at[3])
+
+    def ga2(p):
+        return Exchange(Z, f, along_z, lambda j: rta.at[f, p], lambda i: rta.at[i, p], s_pa.at[1, p], r_pa.at[1, p])
+
+    def gb2(p):
+        return Exchange(Y, r, along_y, lambda j: rtb.at[r, p], lambda i: rtb.at[i, p], s_pb.at[1, p], r_pb.at[1, p])
+
+    ex_qt = Exchange(T, t, along_t, lambda j: sq_t.at[t], lambda i: sq_t.at[i], s_z.at[4], r_z.at[4])
+    ex_qy = Exchange(Y, r, along_y, lambda j: sq_y.at[r], lambda i: sq_y.at[i], s_y.at[2], r_y.at[2])
+    ex_qz = Exchange(Z, f, along_z, lambda j: sq_z.at[f], lambda i: sq_z.at[i], s_z.at[5], r_z.at[5])
 
     loads[0].wait()
     q_h, q_l = split(q_v[...])
@@ -187,10 +209,10 @@
     ex_proj.start()
     ex_proj.wait_recv()
 
-    p = proj[...].reshape(512, 128)
-    pt = p.T
+    p_all = proj[...].reshape(512, 128)
+    pt = p_all.T
     pt_h, pt_l = split(pt)
-    gram_p[...] = mmf(pt, p).reshape(Z, 16, 128)
+    gram_p[...] = mmf(pt, p_all).reshape(Z, 16, 128)
     gram_r[pl.ds(f, 1)] = gram_p[pl.ds(f, 1)]
     ex_gram.start()
 
@@ -199,63 +221,127 @@
         w = mm(pt_h, b_h) + (mm(pt_l, b_h) + mm(pt_h, lo_v[:, lo : lo + n]))
         return w.T
 
+    order_a = [lax.rem(r + o, Y) for o in (2, 1, 3, 0)]
+    order_b = [lax.rem(f + o, Z) for o in (4, 3, 5, 2, 6, 1, 7, 0)]
+
+    def take_a(p, last=False):
+        ex_a1(p).wait_recv()
+        acc = wa[f, p]
+        for o in range(1, Z):
+            acc = acc + ra1[lax.rem(f + o, Z), p]
+        if last:
+            return acc
+        sa1[p] = acc
+        ex_a2.start_one(p)
+
+    def take_b(p, last=False):
+        ex_b1(p).wait_recv()
+        acc = wb[r, p]
+        for o in range(1, Y):
+            acc = acc + rb1[lax.rem(r + o, Y), p]
+        if last:
+            return acc
+        sb1[p] = acc
+        ex_b2.start_one(p)
+
+    wa[...] = columns(0, 512).reshape(Z, Y, 16, 128)
+    for p in order_a[0:2]:
+        ex_a1(p).start()
     for c in range(2):
-        wa[4 * c : 4 * c + 4] = columns(384 * c, 384).reshape(4, 96, 128)
-    ra1[pl.ds(f, 1)] = wa[pl.ds(f, 1)]
-    ex_a1.start()
-    for c in range(2):
-        wb[2 * c : 2 * c + 2] = columns(768 + 640 * c, 640).reshape(2, 320, 128)
-    rb1[pl.ds(r, 1)] = wb[pl.ds(r, 1)]
-    ex_b1.start()
-
+        wb[2 * c : 2 * c + 2] = columns(512 + 768 * c, 768).reshape(2, Z, 48, 128)
+    for p in order_b:
+        ex_b1(p).start()
     ex_gram.wait_recv()
     gram[pl.ds(f, 1)] = total(gram_r, Z)[None]
     ex_gall.start()
-    ex_b1.wait_recv()
-    sb1[...] = total(rb1, Y).reshape(Z, 40, 128)
-    rb2[pl.ds(f, 1)] = sb1[pl.ds(f, 1)]
-    ex_b2.start()
+    for p in order_a[2:4]:
+        ex_a1(p).start()
+
+    for p in order_b[0:2]:
+        take_b(p)
+    take_a(order_a[0])
+    take_b(order_b[2])
     ex_gall.wait_recv()
-    inverse = factor(work, gram[...].reshape(128, 128))
-    ex_a1.wait_recv()
-    sa1[...] = total(ra1, Z).reshape(Y, 24, 128)
-    ra2[pl.ds(r, 1)] = sa1[pl.ds(r, 1)]
-    ex_a2.start()
-    basis_v[...] = mmf(p, inverse, ((1,), (1,)))
+    steps = factor(work, gram[...].reshape(128, 128))
+    next(steps)
+    take_b(order_b[3])
+    take_b(order_b[4])
+    take_a(order_a[1])
+    next(steps)
+    take_b(order_b[5])
+    take_a(order_a[2])
+    next(steps)
+    take_b(order_b[6])
+    own_a = take_a(order_a[3], last=True)
+    next(steps)
+    own_b = take_b(order_b[7], last=True)
+    inverse = inverse_factor(work)
+
+    ex_a2.wait_recv()
+    for o in range(1, Y):
+        own_a = own_a + ra2[lax.rem(r + o, Y)]
+    ex_b2.wait_recv()
+    for o in range(1, Z):
+        own_b = own_b + rb2[lax.rem(f + o, Z)]
+    w = jnp.concatenate([own_a, own_b], axis=0)
+    right = 0.25 * mmf(w, inverse, ((1,), (1,)))
+    rta[f, r] = right[0:16]
+    rtb[r, f] = right[16:64]
+    gb1.start()
+    ga1.start()
+    squares = jnp.sum(right * right, axis=0, keepdims=True)
+    sq_t[t] = jnp.broadcast_to(squares, (8, 128))
+    ex_qt.start()
+    gb2(f).start()
+    ga2(r).start()
+
+    def forward_b(o):
+        p = lax.rem(f + o, Z)
+        gb1.recv_one(p)
+        gb2(p).start()
+
+    for o in (1, 7):
+        forward_b(o)
+    for o in range(1, Y):
+        p = lax.rem(r + o, Y)
+        ga1.recv_one(p)
+        ga2(p).start()
+    ex_qt.wait_recv()
+    sq_y[r] = total(sq_t, T)
+    ex_qy.start()
+    for o in (2, 6, 3, 5, 4):
+        forward_b(o)
+    ex_qy.wait_recv()
+    sq_z[f] = total(sq_y, Y)
+    ex_qz.start()
+    basis_v[...] = mmf(proj[...].reshape(512, 128), inverse, ((1,), (1,)))
     keep_basis = pltpu.make_async_copy(basis_v, basis_out, store.at[0])
     keep_basis.start()
-    ex_a2.wait_recv()
-    ex_b2.wait_recv()
-    w = jnp.concatenate([total(ra2, Y), total(rb2, Z)], axis=0)
-    right = 0.25 * mmf(w, inverse, ((1,), (1,)))
-    rta[pl.ds(f, 1), pl.ds(r, 1)] = right[0:24][None, None]
-    rtb[pl.ds(r, 1), pl.ds(f, 1)] = right[24:64][None, None]
-    ga1.start()
-    gb1.start()
-    squares = jnp.sum(right * right, axis=0, keepdims=True)
-    sq_t[pl.ds(t, 1)] = jnp.broadcast_to(squares, (8, 128))[None]
-    ex_qt.start()
-
-    ex_qt.wait_recv()
-    sq_y[pl.ds(r, 1)] = total(sq_t, T)[None]
-    ex_qy.start()
-    ga1.wait_recv()
-    ga2.start()
-    ex_qy.wait_recv()
-    sq_z[pl.ds(f, 1)] = total(sq_y, Y)[None]
-    ex_qz.start()
-    gb1.wait_recv()
-    gb2.start()
+    for o in range(Z):
+        gb2(lax.rem(f + o, Z)).wait_recv()
+    keep_b = pltpu.make_async_copy(rtb.reshape(1536, 128), right_out.at[512:2048], store.at[1])
+    keep_b.start()
+    for o in range(Y):
+        ga2(lax.rem(r + o, Y)).wait_recv()
+    keep_a = pltpu.make_async_copy(rta.reshape(512, 128), right_out.at[0:512], store.at[2])
+    keep_a.start()
     ex_qz.wait_recv()
     sq_out[...] = total(sq_z, Z)
-    gb2.wait_recv()
-    keep_b = pltpu.make_async_copy(rtb.reshape(1280, 128), right_out.at[768:2048], store.at[1])
-    keep_a = pltpu.make_async_copy(rta.reshape(768, 128), right_out.at[0:768], store.at[2])
-    keep_b.start()
-    ga2.wait_recv()
-    keep_a.start()
-    for ex in (ex_part, ex_proj, ex_gram, ex_gall, ex_a1, ex_b1, ex_a2, ex_b2, ga1, gb1, ga2, gb2, ex_qt, ex_qy, ex_qz):
+    for ex in (ex_part, ex_proj, ex_gram, ex_gall, ex_a2, ex_b2, ga1, gb1, ex_qt, ex_qy, ex_qz):
         ex.wait_send()
+
+    def sent_a(p, carry):
+        ex_a1(p).wait_send()
+        ga2(p).wait_send()
+        return carry
+
+    def sent_b(p, carry):
+        ex_b1(p).wait_send()
+        gb2(p).wait_send()
+        return carry
+
+    lax.fori_loop(0, Y, sent_a, 0)
+    lax.fori_loop(0, Z, sent_b, 0)
     keep_weight.wait()
     keep_buffer.wait()
     keep_basis.wait()
@@ -263,19 +349,30 @@
     keep_a.wait()
 
 
-def finish(buffer, weight, right, basis, sq, weight_out, mom_out, q_out):
-    r = right[...]
+def finish(buffer, weight, right, basis, sq, weight_out, mom_out, q_out, w_v, m_v, q_v, sem_w, sem_m, sem_q):
     scale = lax.rsqrt(sq[0:1] * (1.0 / 16384.0) + 1e-06)
-    q_out[...] = r * scale
-    r_h, r_l = split(r)
     nt = ((1,), (1,))
     b = basis[...]
     b_h, b_l = split(b)
-    feedback = mm(b_h, r_h, nt) + (mm(b_h, r_l, nt) + mm(b_l, r_h, nt))
-    mom_out[...] = buffer[...] - 0.05 * feedback
     s_h, s_l = split(b * scale)
-    update = mm(s_h, r_h, nt) + (mm(s_h, r_l, nt) + mm(s_l, r_h, nt))
-    weight_out[...] = 0.999 * weight[...] - 0.2 * update
+    copies = []
+    for c in range(8):
+        cols = pl.ds(256 * c, 256)
+        r = right[cols, :]
+        r_h, r_l = split(r)
+        feedback = mm(b_h, r_h, nt) + (mm(b_h, r_l, nt) + mm(b_l, r_h, nt))
+        m_v[:, cols] = buffer[:, cols] - 0.05 * feedback
+        copies.append(pltpu.make_async_copy(m_v.at[:, cols], mom_out.at[:, cols], sem_m.at[c]))
+        copies[-1].start()
+        update = mm(s_h, r_h, nt) + (mm(s_h, r_l, nt) + mm(s_l, r_h, nt))
+        w_v[:, cols] = 0.999 * weight[:, cols] - 0.2 * update
+        copies.append(pltpu.make_async_copy(w_v.at[:, cols], weight_out.at[:, cols], sem_w.at[c]))
+        copies[-1].start()
+        q_v[cols, :] = r * scale
+        copies.append(pltpu.make_async_copy(q_v.at[cols, :], q_out.at[cols, :], sem_q.at[c]))
+        copies[-1].start()
+    for cp in copies:
+        cp.wait()
 
 
 def shards(weight, momentum, gradient, q_in):
@@ -300,29 +397,26 @@
             pltpu.VMEM((512, 2048), BF16), pltpu.VMEM((512, 2048), BF16), pltpu.VMEM((2048, 256), BF16),
             vm(G, 16, 128), vm(G, 16, 128), vm(G, 16, 128),
             vm(Z, 16, 128), vm(Z, 16, 128), vm(Z, 16, 128),
-            vm(Z, 96, 128), vm(Y, 320, 128), vm(Z, 96, 128), vm(Y, 320, 128),
-            vm(Y, 24, 128), vm(Z, 40, 128), vm(Y, 24, 128), vm(Z, 40, 128),
-            vm(Z, Y, 24, 128), vm(Y, Z, 40, 128),
+            vm(Z, Y, 16, 128), vm(Y, Z, 48, 128), vm(Z, Y, 16, 128), vm(Y, Z, 48, 128),
+            vm(Y, 16, 128), vm(Z, 48, 128), vm(Y, 16, 128), vm(Z, 48, 128),
+            vm(Z, Y, 16, 128), vm(Y, Z, 48, 128),
             vm(128, 256), vm(512, 128), vm(T, 8, 128), vm(Y, 8, 128), vm(Z, 8, 128),
-            dma(11), dma(3), dma(2, G), dma(2, G), dma(8, Z), dma(8, Z), dma(5, Y), dma(5, Y),
+            dma(11), dma(3), dma(2, G), dma(2, G), dma(6, Z), dma(6, Z), dma(3, Y), dma(3, Y),
+            dma(2, Y, Z), dma(2, Y, Z), dma(2, Z, Y), dma(2, Z, Y),
         ],
         compiler_params=pltpu.CompilerParams(collective_id=0, has_side_effects=True, vmem_limit_bytes=28 << 20),
         cost_estimate=pl.CostEstimate(flops=1 << 31, bytes_accessed=8 << 20, transcendentals=0),
     )(*(pltpu.with_memory_space_constraint(x, pltpu.HBM) for x in (mom, grad, q_in, weight)))
-    n = 512
-    wide = pl.BlockSpec((512, n), lambda i: (0, i))
-    tall = pl.BlockSpec((n, 128), lambda i: (i, 0))
-    whole = lambda rows: pl.BlockSpec((rows, 128), lambda i: (0, 0))
     weight_new, momentum_new, q_new = pl.pallas_call(
         finish,
-        grid=(2048 // n,),
         out_shape=(
             jax.ShapeDtypeStruct((512, 2048), F32),
             jax.ShapeDtypeStruct((512, 2048), F32),
             jax.ShapeDtypeStruct((2048, 128), F32),
         ),
-        in_specs=[wide, wide, tall, whole(512), whole(8)],
-        out_specs=(wide, wide, tall),
+        in_specs=[pl.BlockSpec(memory_space=pltpu.VMEM)] * 5,
+        out_specs=(any_, any_, any_),
+        scratch_shapes=[vm(512, 2048), vm(512, 2048), vm(2048, 128), dma(8), dma(8), dma(8)],
         compiler_params=pltpu.CompilerParams(vmem_limit_bytes=24 << 20),
         cost_estimate=pl.CostEstimate(flops=1 << 31, bytes_accessed=21 << 20, transcendentals=0),
     )(buffer, weight, right, basis, sq)

time: 76 us -> 71.5 us (0.941)
  Pallas kernels: 74.3 us -> 69.6 us
    pallas_call x1, Pallas kernels: 68.6 us -> 64.7 us  [shards(): pl.pallas_call(talk, out_shape=(jax.ShapeDtypeStruct((2048, 128), F32), j...]
where the time goes in v3:
time: 71.5 us; the launch traced here: 70.2 us
  Pallas kernels  69.6 us (97%)
    pallas_call x1, Pallas kernels, shards(): pl.pallas_call(talk, out_shape=(jax.ShapeDtypeStruct((2048, 128), F32), j...  64.7 us
    pallas_call x1, Pallas kernels, shards(): pl.pallas_call(finish, out_shape=(jax.ShapeDtypeStruct((512, 2048), F32),...  4.93 us

profile of v3, /device:TPU:32, one launch (start us, length us, event | category | flops | bytes accessed | tf_op | source)
XLA Modules:
  0.0 70.2 jit_solution(12654816319737771333)
XLA Ops:
  0.6 64.7 %shard_map.67 = (f32[2048,128]{1,0:T(8,128)S(1)}, f32[512,128]{1,0:T(8,128)S(1)}, f32[8,128]{1,0:T(8,128)S(1)}, f32[512,2048]{1,0:T(8,128)S(1)}, f32[512,2048]{1,0:T(8,128)S(1)}) custom-call(f32[512,2048]{1,0:T(8,128)} %bitcast.3, bf16[512,2048]{1,0:T(8,128)(2,1)} %bitcast.4, f32[2048,128]{1,0:T(8,128)} %q_in.1, f32[512,2048]{1,0:T(8,128)} %weight.1), custom_call_target="tpu_custom_call" | custom-call | flops 2147483648 | bytes 8388608 | tf_op jit(solution)/shard_map/pallas_call | solution.py:384
  65.3 4.9 %shard_map.68 = (f32[512,2048]{1,0:T(8,128)}, f32[512,2048]{1,0:T(8,128)}, f32[2048,128]{1,0:T(8,128)}) custom-call(f32[512,2048]{1,0:T(8,128)S(1)} %get-tuple-element.11.buffer, f32[512,2048]{1,0:T(8,128)S(1)} %get-tuple-element.12.weight, f32[2048,128]{1,0:T(8,128)S(1)} %get-tuple-element.13.right, f32[512,128]{1,0:T(8,128)S(1)} %get-tuple-element.14.basis, ...), custom_call_target="tpu_custom_call" | custom-call | flops 2147483648 | bytes 22020096 | tf_op jit(solution)/shard_map/pallas_call | solution.py:410

commit v4 on v3

--- a/solution.py
+++ b/solution.py
@@ -35,7 +35,7 @@
             body(lax.rem(self.me + o, self.n))
             return carry
 
-        lax.fori_loop(1, self.n, step, 0)
+        lax.fori_loop(1, self.n, step, 0, unroll=True)
 
     def copy(self, j, slot):
         return pltpu.make_async_remote_copy(
@@ -121,7 +121,7 @@
     mom_v, grad_v, q_v, hi_v, lo_v, q_hl,
     part, part_r, proj, gram_p, gram_r, gram,
     wa, wb, ra1, rb1, sa1, sb1, ra2, rb2, rta, rtb,
-    work, basis_v, sq_t, sq_y, sq_z,
+    work, basis_v, sq_p, sq_z,
     load, store, s_tp, r_tp, s_z, r_z, s_y, r_y, s_pa, r_pa, s_pb, r_pb,
 ):
     f, t, r = lax.axis_index("fsdp"), lax.axis_index("tp"), lax.axis_index("rep")
@@ -139,7 +139,6 @@
     plane = lambda j: {"tp": lax.div(j, Y), "rep": lax.rem(j, Y)}
     along_z = lambda j: {"fsdp": j}
     along_y = lambda j: {"rep": j}
-    along_t = lambda j: {"tp": j}
 
     barrier = pltpu.get_barrier_semaphore()
 
@@ -175,9 +174,8 @@
     def gb2(p):
         return Exchange(Y, r, along_y, lambda j: rtb.at[r, p], lambda i: rtb.at[i, p], s_pb.at[1, p], r_pb.at[1, p])
 
-    ex_qt = Exchange(T, t, along_t, lambda j: sq_t.at[t], lambda i: sq_t.at[i], s_z.at[4], r_z.at[4])
-    ex_qy = Exchange(Y, r, along_y, lambda j: sq_y.at[r], lambda i: sq_y.at[i], s_y.at[2], r_y.at[2])
-    ex_qz = Exchange(Z, f, along_z, lambda j: sq_z.at[f], lambda i: sq_z.at[i], s_z.at[5], r_z.at[5])
+    ex_qp = Exchange(G, g, plane, lambda j: sq_p.at[g], lambda i: sq_p.at[i], s_tp.at[2], r_tp.at[2])
+    ex_qz = Exchange(Z, f, along_z, lambda j: sq_z.at[f], lambda i: sq_z.at[i], s_z.at[4], r_z.at[4])
 
     loads[0].wait()
     q_h, q_l = split(q_v[...])
@@ -290,8 +288,8 @@
     gb1.start()
     ga1.start()
     squares = jnp.sum(right * right, axis=0, keepdims=True)
-    sq_t[t] = jnp.broadcast_to(squares, (8, 128))
-    ex_qt.start()
+    sq_p[g] = jnp.broadcast_to(squares, (8, 128))
+    ex_qp.start()
     gb2(f).start()
     ga2(r).start()
 
@@ -300,20 +298,23 @@
         gb1.recv_one(p)
         gb2(p).start()
 
-    for o in (1, 7):
-        forward_b(o)
-    for o in range(1, Y):
+    def forward_a(o):
         p = lax.rem(r + o, Y)
         ga1.recv_one(p)
         ga2(p).start()
-    ex_qt.wait_recv()
-    sq_y[r] = total(sq_t, T)
-    ex_qy.start()
-    for o in (2, 6, 3, 5, 4):
+
+    for o in (1, 7):
         forward_b(o)
-    ex_qy.wait_recv()
-    sq_z[f] = total(sq_y, Y)
+    forward_a(1)
+    forward_a(3)
+    forward_a(2)
+    forward_b(2)
+    forward_b(6)
+    ex_qp.wait_recv()
+    sq_z[f] = total(sq_p, G)
     ex_qz.start()
+    for o in (3, 5, 4):
+        forward_b(o)
     basis_v[...] = mmf(proj[...].reshape(512, 128), inverse, ((1,), (1,)))
     keep_basis = pltpu.make_async_copy(basis_v, basis_out, store.at[0])
     keep_basis.start()
@@ -327,7 +328,7 @@
     keep_a.start()
     ex_qz.wait_recv()
     sq_out[...] = total(sq_z, Z)
-    for ex in (ex_part, ex_proj, ex_gram, ex_gall, ex_a2, ex_b2, ga1, gb1, ex_qt, ex_qy, ex_qz):
+    for ex in (ex_part, ex_proj, ex_gram, ex_gall, ex_a2, ex_b2, ga1, gb1, ex_qp, ex_qz):
         ex.wait_send()
 
     def sent_a(p, carry):
@@ -400,8 +401,8 @@
             vm(Z, Y, 16, 128), vm(Y, Z, 48, 128), vm(Z, Y, 16, 128), vm(Y, Z, 48, 128),
             vm(Y, 16, 128), vm(Z, 48, 128), vm(Y, 16, 128), vm(Z, 48, 128),
             vm(Z, Y, 16, 128), vm(Y, Z, 48, 128),
-            vm(128, 256), vm(512, 128), vm(T, 8, 128), vm(Y, 8, 128), vm(Z, 8, 128),
-            dma(11), dma(3), dma(2, G), dma(2, G), dma(6, Z), dma(6, Z), dma(3, Y), dma(3, Y),
+            vm(128, 256), vm(512, 128), vm(G, 8, 128), vm(Z, 8, 128),
+            dma(11), dma(3), dma(3, G), dma(3, G), dma(5, Z), dma(5, Z), dma(2, Y), dma(2, Y),
             dma(2, Y, Z), dma(2, Y, Z), dma(2, Z, Y), dma(2, Z, Y),
         ],
         compiler_params=pltpu.CompilerParams(collective_id=0, has_side_effects=True, vmem_limit_bytes=28 << 20),

time: 71.5 us -> 66.2 us (0.926); the launches traced: 70.2 us -> 66.1 us
  Pallas kernels: 69.6 us -> 65.5 us
    pallas_call x1, Pallas kernels: 64.7 us -> 60.6 us  [shards(): pl.pallas_call(talk, out_shape=(jax.ShapeDtypeStruct((2048, 128), F32), j...]
where the time goes in v4:
time: 66.2 us; the launch traced here: 66.1 us
  Pallas kernels  65.5 us (99%)
    pallas_call x1, Pallas kernels, shards(): pl.pallas_call(talk, out_shape=(jax.ShapeDtypeStruct((2048, 128), F32), j...  60.6 us
    pallas_call x1, Pallas kernels, shards(): pl.pallas_call(finish, out_shape=(jax.ShapeDtypeStruct((512, 2048), F32),...  4.94 us

profile of v4, /device:TPU:32, one launch (start us, length us, event | category | flops | bytes accessed | tf_op | source)
XLA Modules:
  0.0 66.1 jit_solution(5766901033437793798)
XLA Ops:
  0.6 60.6 %shard_map.67 = (f32[2048,128]{1,0:T(8,128)S(1)}, f32[512,128]{1,0:T(8,128)S(1)}, f32[8,128]{1,0:T(8,128)S(1)}, f32[512,2048]{1,0:T(8,128)S(1)}, f32[512,2048]{1,0:T(8,128)S(1)}) custom-call(f32[512,2048]{1,0:T(8,128)} %bitcast.3, bf16[512,2048]{1,0:T(8,128)(2,1)} %bitcast.4, f32[2048,128]{1,0:T(8,128)} %q_in.1, f32[512,2048]{1,0:T(8,128)} %weight.1), custom_call_target="tpu_custom_call" | custom-call | flops 2147483648 | bytes 8388608 | tf_op jit(solution)/shard_map/pallas_call | solution.py:385
  61.2 4.9 %shard_map.68 = (f32[512,2048]{1,0:T(8,128)}, f32[512,2048]{1,0:T(8,128)}, f32[2048,128]{1,0:T(8,128)}) custom-call(f32[512,2048]{1,0:T(8,128)S(1)} %get-tuple-element.11.buffer, f32[512,2048]{1,0:T(8,128)S(1)} %get-tuple-element.12.weight, f32[2048,128]{1,0:T(8,128)S(1)} %get-tuple-element.13.right, f32[512,128]{1,0:T(8,128)S(1)} %get-tuple-element.14.basis, ...), custom_call_target="tpu_custom_call" | custom-call | flops 2147483648 | bytes 22020096 | tf_op jit(solution)/shard_map/pallas_call | solution.py:411

commit v5 on v4

--- a/solution.py
+++ b/solution.py
@@ -31,11 +31,9 @@
         self.send, self.recv = send, recv
 
     def each(self, body):
-        def step(o, carry):
+        order = {Z: (4, 3, 5, 2, 6, 1, 7), Y: (2, 1, 3)}.get(self.n, range(1, self.n))
+        for o in order:
             body(lax.rem(self.me + o, self.n))
-            return carry
-
-        lax.fori_loop(1, self.n, step, 0, unroll=True)
 
     def copy(self, j, slot):
         return pltpu.make_async_remote_copy(
@@ -310,11 +308,11 @@
     forward_a(2)
     forward_b(2)
     forward_b(6)
+    for o in (3, 5, 4):
+        forward_b(o)
     ex_qp.wait_recv()
     sq_z[f] = total(sq_p, G)
     ex_qz.start()
-    for o in (3, 5, 4):
-        forward_b(o)
     basis_v[...] = mmf(proj[...].reshape(512, 128), inverse, ((1,), (1,)))
     keep_basis = pltpu.make_async_copy(basis_v, basis_out, store.at[0])
     keep_basis.start()

time: 66.2 us -> 65.6 us (level); the launches traced: 66.1 us -> 64.5 us
  Pallas kernels: 65.5 us -> 63.9 us
    pallas_call x1, Pallas kernels: 60.6 us -> 58.9 us  [shards(): pl.pallas_call(talk, out_shape=(jax.ShapeDtypeStruct((2048, 128), F32), j...]
where the time goes in v5:
time: 65.6 us; the launch traced here: 64.5 us
  Pallas kernels  63.9 us (97%)
    pallas_call x1, Pallas kernels, shards(): pl.pallas_call(talk, out_shape=(jax.ShapeDtypeStruct((2048, 128), F32), j...  58.9 us
    pallas_call x1, Pallas kernels, shards(): pl.pallas_call(finish, out_shape=(jax.ShapeDtypeStruct((512, 2048), F32),...  4.94 us

profile of v5, /device:TPU:32, one launch (start us, length us, event | category | flops | bytes accessed | tf_op | source)
XLA Modules:
  0.0 64.5 jit_solution(3392316599208258186)
XLA Ops:
  0.6 58.9 %shard_map.67 = (f32[2048,128]{1,0:T(8,128)S(1)}, f32[512,128]{1,0:T(8,128)S(1)}, f32[8,128]{1,0:T(8,128)S(1)}, f32[512,2048]{1,0:T(8,128)S(1)}, f32[512,2048]{1,0:T(8,128)S(1)}) custom-call(f32[512,2048]{1,0:T(8,128)} %bitcast.3, bf16[512,2048]{1,0:T(8,128)(2,1)} %bitcast.4, f32[2048,128]{1,0:T(8,128)} %q_in.1, f32[512,2048]{1,0:T(8,128)} %weight.1), custom_call_target="tpu_custom_call" | custom-call | flops 2147483648 | bytes 8388608 | tf_op jit(solution)/shard_map/pallas_call | solution.py:383
  59.6 4.9 %shard_map.68 = (f32[512,2048]{1,0:T(8,128)}, f32[512,2048]{1,0:T(8,128)}, f32[2048,128]{1,0:T(8,128)}) custom-call(f32[512,2048]{1,0:T(8,128)S(1)} %get-tuple-element.11.buffer, f32[512,2048]{1,0:T(8,128)S(1)} %get-tuple-element.12.weight, f32[2048,128]{1,0:T(8,128)S(1)} %get-tuple-element.13.right, f32[512,128]{1,0:T(8,128)S(1)} %get-tuple-element.14.basis, ...), custom_call_target="tpu_custom_call" | custom-call | flops 2147483648 | bytes 22020096 | tf_op jit(solution)/shard_map/pallas_call | solution.py:409
